TPU v7x, 512 devices: a whole 4x4x16 slice. The times are simulated.
512 devices in a mesh: ch: 512 (over x, y, z, core).
Axes of the slice: x: 4, y: 4, z: 16, core: 2. Of those that a mesh axis runs over, the one named last changes fastest.
Arguments:
- strain: bfloat16 [8192, 6144], P('ch'), may hold values from -12 to 12
- band_start: int32 [1], replicated, may hold values from 0 to 255
- sketch_seed: int32 [1], replicated, may hold values from 0 to 999999
Outputs:
- modes: float32 [8192, 2, 16, 128], P('ch')
- factor: float32 [2, 16, 16, 128], replicated
All inputs are finite; a program needn't handle non-finite values.
Results may differ from a plain program's by a relative error of at most 0.0003.
The roundings to bfloat16 on the way count: a program that leaves them out, or rounds other values in their place, can miss the bound.
Values sent between devices are 32-bit elements; how exact they have to be, the bound alone decides.
A program may use at most 64 MiB of HBM per device.

v0:
```python
import math

import jax
import jax.numpy as jnp
from jax import lax
from jax.sharding import PartitionSpec as P

SEGMENTS = 24
LINES = 128
SKETCH = 16


def dft_table(band_start, segment_length, line_count):
    times_idx = jnp.arange(segment_length, dtype=jnp.int32)[:, None]
    line_ids = band_start[0] + jnp.arange(line_count, dtype=jnp.int32)[None, :]
    residues = times_idx * line_ids % segment_length
    phases = 2.0 * math.pi / segment_length * residues.astype(jnp.float32)
    window = 0.5 - 0.5 * jnp.cos(2.0 * math.pi / segment_length * times_idx.astype(jnp.float32))
    weighting = window / math.sqrt(3.0 * segment_length / 8.0)
    return jnp.concatenate(
        [weighting * jnp.cos(phases), -weighting * jnp.sin(phases)], axis=1
    ).astype(jnp.bfloat16)


def sketch_signs(first_channel, count, sketch_seed, sketch):
    channel_ids = first_channel + jnp.arange(count, dtype=jnp.int32)[:, None, None]
    column_ids = jnp.arange(sketch, dtype=jnp.int32)[None, :, None]
    halves = jnp.arange(2, dtype=jnp.int32)[None, None, :]
    hashed = (channel_ids * sketch + column_ids) * 2 + halves + sketch_seed[0] * 1000003
    hashed = hashed * -1640531535
    hashed = jnp.bitwise_xor(hashed, lax.shift_right_logical(hashed, jnp.full_like(hashed, 15)))
    hashed = hashed * 2146121005
    hashed = jnp.bitwise_xor(hashed, lax.shift_right_logical(hashed, jnp.full_like(hashed, 13)))
    sign_bits = jnp.bitwise_and(lax.shift_right_logical(hashed, jnp.full_like(hashed, 7)), 1)
    signs = (1 - 2 * sign_bits).astype(jnp.float32)
    return (signs[:, :, 0], signs[:, :, 1])


def contract(form, left_re, left_im, right_re, right_im, conjugate):

    def product(left, right):
        return jnp.einsum(form, left, right, precision=lax.Precision.HIGHEST)

    if conjugate:
        return (
            product(left_re, right_re) + product(left_im, right_im),
            product(left_re, right_im) - product(left_im, right_re),
        )
    return (
        product(left_re, right_re) - product(left_im, right_im),
        product(left_re, right_im) + product(left_im, right_re),
    )


def cholesky_upper(gram_re, gram_im):
    size = gram_re.shape[0]
    column_ids = jnp.arange(size, dtype=jnp.int32)[:, None]
    rows_re = []
    rows_im = []
    for column in range(size):
        accum_re = gram_re[column]
        accum_im = gram_im[column]
        if column > 0:
            prior_re = jnp.stack(rows_re)
            prior_im = jnp.stack(rows_im)
            top_re = prior_re[:, column, :][:, None, :]
            top_im = prior_im[:, column, :][:, None, :]
            accum_re = accum_re - jnp.sum(top_re * prior_re + top_im * prior_im, axis=0)
            accum_im = accum_im - jnp.sum(top_re * prior_im - top_im * prior_re, axis=0)
        diagonal = jnp.sqrt(accum_re[column])
        beyond = column_ids > column
        row_re = jnp.where(beyond, accum_re / diagonal[None, :], 0.0)
        row_re = jnp.where(column_ids == column, diagonal[None, :], row_re)
        row_im = jnp.where(beyond, accum_im / diagonal[None, :], 0.0)
        rows_re.append(row_re)
        rows_im.append(row_im)
    return (jnp.stack(rows_re), jnp.stack(rows_im))


def upper_inverse(upper_re, upper_im):
    size = upper_re.shape[0]
    column_ids = jnp.arange(size, dtype=jnp.int32)[:, None]
    lines = upper_re.shape[2]
    inverse_re = [None] * size
    inverse_im = [None] * size
    for across in range(size - 1, -1, -1):
        accum_re = jnp.broadcast_to(
            jnp.where(column_ids == across, 1.0, 0.0), (size, lines)
        ).astype(jnp.float32)
        accum_im = jnp.zeros((size, lines), jnp.float32)
        if across < size - 1:
            later_re = jnp.stack(inverse_re[across + 1 :])
            later_im = jnp.stack(inverse_im[across + 1 :])
            coef_re = upper_re[across, across + 1 :, :][:, None, :]
            coef_im = upper_im[across, across + 1 :, :][:, None, :]
            accum_re = accum_re - jnp.sum(coef_re * later_re - coef_im * later_im, axis=0)
            accum_im = accum_im - jnp.sum(coef_re * later_im + coef_im * later_re, axis=0)
        pivot_value = upper_re[across, across][None, :]
        inverse_re[across] = accum_re / pivot_value
        inverse_im[across] = accum_im / pivot_value
    return (jnp.stack(inverse_re), jnp.stack(inverse_im))


def shards(strain, band_start, sketch_seed):
    channel_count = strain.shape[0]
    segment_length = strain.shape[1] // SEGMENTS
    channels_all = channel_count * lax.axis_size("ch")
    scaling = 1.0 / (SEGMENTS * channels_all)
    table = dft_table(band_start, segment_length, LINES)
    flat_rows = strain.reshape(channel_count * SEGMENTS, segment_length)
    spectra = jnp.dot(flat_rows, table, preferred_element_type=jnp.float32)
    spectra = spectra.reshape(channel_count, SEGMENTS, 2, LINES)
    spec_re = spectra[:, :, 0, :]
    spec_im = spectra[:, :, 1, :]
    first_channel = lax.axis_index("ch") * channel_count
    sign_re, sign_im = sketch_signs(first_channel, channel_count, sketch_seed, SKETCH)
    sketch_re, sketch_im = contract("csf,ck->skf", spec_re, spec_im, sign_re, sign_im, True)
    sketch_re, sketch_im = lax.psum((sketch_re, sketch_im), "ch")
    first_re, first_im = contract("csf,skf->ckf", spec_re, spec_im, sketch_re, sketch_im, False)
    power_re, power_im = contract(
        "csf,ckf->skf", spec_re, spec_im, first_re * scaling, first_im * scaling, True
    )
    power_re, power_im = lax.psum((power_re, power_im), "ch")
    basis_re, basis_im = contract("csf,skf->ckf", spec_re, spec_im, power_re, power_im, False)
    basis_re = basis_re * scaling
    basis_im = basis_im * scaling
    gram_re, gram_im = contract("cjf,ckf->jkf", basis_re, basis_im, basis_re, basis_im, True)
    gram_re, gram_im = lax.psum((gram_re, gram_im), "ch")
    factor_re, factor_im = cholesky_upper(gram_re, gram_im)
    inverse_re, inverse_im = upper_inverse(factor_re, factor_im)
    modes_re, modes_im = contract("cjf,jkf->ckf", basis_re, basis_im, inverse_re, inverse_im, False)
    root = math.sqrt(channels_all)
    modes = jnp.stack([modes_re * root, modes_im * root], axis=1)
    factor = jnp.stack([factor_re, factor_im], axis=0)
    return (modes, factor)


def solution(mesh):
    in_specs = (P("ch", None), P(), P())
    out_specs = (P("ch", None, None, None), P())
    return jax.shard_map(shards, mesh=mesh, in_specs=in_specs, out_specs=out_specs, check_vma=False)
```

profile of v0, /device:TPU:1, one launch (start us, length us, event | category | flops | bytes accessed | tf_op | source)
XLA Modules:
  0.0 1557.9 jit_solution(14360096483825352527)
XLA Ops:
  28.8 455.7 %all-reduce.11.cloned.1.call-done = (f32[24,16,128]{2,1,0:T(8,128)}, f32[24,16,128]{2,1,0:T(8,128)}) async-done(((f32[24,16,128]{2,1,0:T(8,128)}, f32[24,16,128]{2,1,0:T(8,128)}), (f32[24,16,128]{2,1,0:T(8,128)}, f32[24,16,128]{2,1,0:T(8,128)})) %all-reduce.11.cloned.1.call-update) | async-done | bytes 393232 | tf_op jit(solution)/shard_map/psum | solution.py:118
  484.5 1.5 copy.4000
  486.0 1.4 copy.4002
  487.4 3.0 fusion.28
  490.4 1.8 fusion.32
  492.2 1.8 fusion.11
  494.0 1.8 fusion.13
  495.8 1.1 fusion.30
  496.9 1.2 fusion.24
  498.1 2.4 fusion.9
  500.5 2.2 fusion.8
  503.9 474.3 %all-reduce.9.cloned.1.call-done = (f32[24,16,128]{0,1,2:T(8,128)}, f32[24,16,128]{0,1,2:T(8,128)}) async-done(((f32[24,16,128]{0,1,2:T(8,128)}, f32[24,16,128]{0,1,2:T(8,128)}), (f32[24,16,128]{0,1,2:T(8,128)}, f32[24,16,128]{0,1,2:T(8,128)})) %all-reduce.9.cloned.1.call-update) | async-done | bytes 393232 | tf_op jit(solution)/shard_map/psum | solution.py:123
  978.2 3.1 fusion.26
  981.3 1.8 fusion.22
  983.2 1.8 fusion.7
  985.0 1.8 fusion.5
  986.7 2.7 fusion.192
  989.5 2.8 fusion.191
  992.2 2.7 fusion.190
  995.0 2.0 fusion.189
  997.0 1.6 copy.4023
  998.6 1.6 copy.4022
  1000.2 1.6 copy.4019
  1005.7 452.5 %all-reduce.7.cloned.1.call-done = (f32[16,16,128]{2,1,0:T(8,128)}, f32[16,16,128]{2,1,0:T(8,128)}) async-done(((f32[16,16,128]{2,1,0:T(8,128)}, f32[16,16,128]{2,1,0:T(8,128)}), (f32[16,16,128]{2,1,0:T(8,128)}, f32[16,16,128]{2,1,0:T(8,128)})) %all-reduce.7.cloned.1.call-update) | async-done | bytes 262160 | tf_op jit(solution)/shard_map/psum | solution.py:128
  1462.2 1.4 slice_bitcast_fusion.27
  1473.1 1.3 slice.548
  1539.2 1.4 copy.4150
  1541.1 1.4 fusion.193
  1542.6 1.2 fusion.194
  1543.8 1.2 fusion.3
  1545.0 2.2 fusion.1
  1547.2 1.6 copy.4157
  (679 shorter events, 104.9 us)
Async XLA Ops:
  7.2 477.3 %all-reduce.11.cloned.1.call-start = ((), (), s32[]{:S(2)}) async-start(), calls=%async_computation.2 | async-start | bytes 786432 | tf_op jit(solution)/shard_map/psum | solution.py:118
  13.8 964.5 %all-reduce.9.cloned.1.call-start = ((), (), s32[]{:S(2)}) async-start(), calls=%async_computation.1 | async-start | bytes 4194304 | tf_op jit(solution)/shard_map/psum | solution.py:123
  484.5 1.5 copy-start.6
  492.2 1.8 copy-start
  502.7 955.6 %all-reduce.7.cloned.1.call-start = ((), (), s32[]{:S(2)}) async-start(), calls=%async_computation | async-start | bytes 524288 | tf_op jit(solution)/shard_map/psum | solution.py:128
  978.2 3.1 copy-start.3
  983.1 1.8 copy-start.2
  1461.0 2.6 copy-start.9
  1466.4 1.4 copy-start.5
  1476.0 2.4 copy-start.25
  1484.6 2.5 copy-start.23
  1489.7 2.5 copy-start.21
  1489.7 4.4 copy-start.86
  1489.7 4.4 copy-start.87
  1493.9 3.8 copy-start.84
  1493.9 3.8 copy-start.85
  1494.1 2.0 copy-start.19
  1494.2 40.7 %copy-start.31 = (f32[128]{0:T(128)}, f32[128]{0:T(128)S(1)}, u32[]{:S(2)}) copy-start(f32[128]{0:T(128)S(1)} %slice_bitcast_fusion.49) | copy-start | bytes 1540
  1494.8 1.9 copy-start.18
  1497.7 2.0 copy-start.17
  1497.7 3.7 copy-start.82
  1497.7 3.7 copy-start.83
  1497.8 2.5 copy-start.16
  1497.8 37.2 %copy-start.28 = (f32[128]{0:T(128)}, f32[128]{0:T(128)S(1)}, u32[]{:S(2)}) copy-start(f32[128]{0:T(128)S(1)} %slice_bitcast_fusion.50) | copy-start | bytes 1540
  1501.4 2.0 copy-start.15
  1501.5 2.5 copy-start.14
  1504.9 1.6 copy-start.13
  1504.9 3.2 copy-start.78
  1504.9 3.2 copy-start.79
  1505.7 1.4 copy-start.12
  1515.1 1.6 copy-start.7
  1541.1 1.4 copy-start.1
  (74 other events, 50.9 us)
Sparse Core Ops, SparseCore 0:
  13.9 470.5 all-reduce.10
  502.8 475.4 all-reduce.8
  1004.7 453.4 all-reduce.6
where the time goes:
time: 1560 us
  waiting for transfers between devices  1380 us (88%)
  local copies, waits for them, and re-layouts  82 us (5%)
  matrix products  42.7 us (3%)
  other arithmetic  32.8 us (2%)
  between operations  17.1 us (1%)
    psum x1, waiting for transfers between devices, shards(): power_re, power_im = lax.psum((power_re, power_im), 'ch')  474 us
    psum x1, waiting for transfers between devices, shards(): sketch_re, sketch_im = lax.psum((sketch_re, sketch_im), 'ch')  456 us
    psum x1, waiting for transfers between devices, shards(): gram_re, gram_im = lax.psum((gram_re, gram_im), 'ch')  453 us
    dot_general x24, matrix products, product(): return jnp.einsum(form, left, right, precision=lax.Precision.HIGHEST)  42.4 us
    unnamed x330, local copies, waits for them, and re-layouts  41.8 us
  transfers between devices with their start and end apart: 3, of which 3 were waited for; matrix products, arithmetic and copies ran while one was open for 1% of the time, Pallas kernels for 0%

commit v1 on v0

v1 whole, which is shorter than its diff:
```python
import functools
import math

import jax
import jax.numpy as jnp
from jax import lax
from jax.experimental import pallas as pl
from jax.experimental.pallas import tpu as pltpu
from jax.sharding import PartitionSpec as P

SEGMENTS = 24
LINES = 128
SKETCH = 16
HALF_ROWS = SEGMENTS * 2 * SKETCH
MESH = pl.DeviceIdType.MESH


def dft_table(band_start, segment_length, line_count):
    times_idx = jnp.arange(segment_length, dtype=jnp.int32)[:, None]
    line_ids = band_start[0] + jnp.arange(line_count, dtype=jnp.int32)[None, :]
    residues = times_idx * line_ids % segment_length
    phases = 2.0 * math.pi / segment_length * residues.astype(jnp.float32)
    window = 0.5 - 0.5 * jnp.cos(2.0 * math.pi / segment_length * times_idx.astype(jnp.float32))
    weighting = window / math.sqrt(3.0 * segment_length / 8.0)
    return jnp.concatenate(
        [weighting * jnp.cos(phases), -weighting * jnp.sin(phases)], axis=1
    ).astype(jnp.bfloat16)


def sign_block(first_channel, seed, channels, copies):
    shape = (2 * SKETCH, copies * channels)
    row = lax.broadcasted_iota(jnp.int32, shape, 0)
    col = lax.broadcasted_iota(jnp.int32, shape, 1)
    channel = first_channel + jnp.bitwise_and(col, channels - 1)
    half = (row >= SKETCH).astype(jnp.int32)
    column = row - half * SKETCH
    hashed = (channel * SKETCH + column) * 2 + half + seed * 1000003
    hashed = hashed * -1640531535
    hashed = jnp.bitwise_xor(hashed, lax.shift_right_logical(hashed, jnp.full_like(hashed, 15)))
    hashed = hashed * 2146121005
    hashed = jnp.bitwise_xor(hashed, lax.shift_right_logical(hashed, jnp.full_like(hashed, 13)))
    bits = jnp.bitwise_and(lax.shift_right_logical(hashed, jnp.full_like(hashed, 7)), 1)
    return (1 - 2 * bits).astype(jnp.float32)


def gram_row(t, s, part):
    block = t // 8
    return 8 * (0, 16, 48)[block] + (t % 8) * 16 * (block + 1) + part * 8 * (block + 1) + s


def sum_kernel(dims, strain, table, seed, full_out, sre, sim,
               part, crecv, xrecv, zflat, zbuf, zrecv, zgat, full,
               c_send, c_recv, x_send, x_recv, z_send, z_recv, g_send, g_recv, a_send, a_recv, f_send, f_recv):
    nx, ny, nz = dims
    planes = nx * ny
    rows = HALF_ROWS // planes
    zrows = rows // nz
    channels = strain.shape[0]
    length = table.shape[0]

    me = lax.axis_index("ch")
    core = lax.rem(me, 2)
    z = lax.rem(lax.div(me, 2), nz)
    p = lax.div(me, 2 * nz)
    x, y = lax.div(p, ny), lax.rem(p, ny)
    mate = me + 1 - 2 * core

    def plane_at(d, sign):
        dx, dy = d // ny, d % ny
        qx = lax.rem(x + (dx if sign > 0 else nx - dx), nx)
        qy = lax.rem(y + (dy if sign > 0 else ny - dy), ny)
        return qx * ny + qy

    def plane_device(q):
        return q * (2 * nz) + z * 2 + core

    def z_at(d):
        return lax.rem(z + d, nz)

    def z_device(k):
        return p * (2 * nz) + k * 2 + core

    barrier = pltpu.get_barrier_semaphore()
    pl.semaphore_signal(barrier, inc=1, device_id=(mate,), device_id_type=MESH)
    for d in range(1, planes):
        pl.semaphore_signal(barrier, inc=1, device_id=(plane_device(plane_at(d, 1)),), device_id_type=MESH)
    for d in range(1, nz):
        pl.semaphore_signal(barrier, inc=1, device_id=(z_device(z_at(d)),), device_id_type=MESH)

    for s in range(SEGMENTS):
        both = jnp.dot(strain[:, s * length:(s + 1) * length], table[...], preferred_element_type=jnp.float32)
        sre[s * channels:(s + 1) * channels, :] = both[:, :LINES]
        sim[s * channels:(s + 1) * channels, :] = both[:, LINES:]

    signs = sign_block(me * channels, seed[0], channels, 3).astype(jnp.bfloat16)
    for s in range(SEGMENTS):
        both = jnp.concatenate([sre[s * channels:(s + 1) * channels, :], sim[s * channels:(s + 1) * channels, :]], axis=1)
        high = both.astype(jnp.bfloat16)
        rest = both - high.astype(jnp.float32)
        middle = rest.astype(jnp.bfloat16)
        low = (rest - middle.astype(jnp.float32)).astype(jnp.bfloat16)
        terms = jnp.concatenate([high, middle, low], axis=0)
        prod = jnp.dot(signs, terms, preferred_element_type=jnp.float32)
        for half, value in enumerate((
            prod[:SKETCH, :LINES] + prod[SKETCH:, LINES:],
            prod[SKETCH:, :LINES] - prod[:SKETCH, LINES:],
        )):
            row = s * 2 * SKETCH + half * SKETCH
            part[0, row // rows, row % rows:row % rows + SKETCH, :] = value

    for t0 in range(0, SEGMENTS, 4):
        n = 8 * (t0 // 8 + 1)

        def step(i, accs, t0=t0, n=n):
            accs = list(accs)
            for k in range(4):
                c = i * 4 + k
                vre = sre[pl.ds(c, n, stride=channels), :]
                vim = sim[pl.ds(c, n, stride=channels), :]
                for a in range(4):
                    bre = sre[pl.ds((t0 + a) * channels + c, 1), :]
                    bim = sim[pl.ds((t0 + a) * channels + c, 1), :]
                    accs[2 * a] += vre * bre + vim * bim
                    accs[2 * a + 1] += vre * bim - vim * bre
            return tuple(accs)

        zero = jnp.zeros((n, LINES), jnp.float32)
        accs = lax.fori_loop(0, channels // 4, step, (zero,) * 8)
        for a in range(4):
            for half in range(2):
                for tile in range(n // 8):
                    row = gram_row(t0 + a, 8 * tile, half)
                    part[1, row // rows, row % rows:row % rows + 8, :] = accs[2 * a + half][8 * tile:8 * tile + 8, :]

    pl.semaphore_wait(barrier, planes + nz - 1)

    def remote(src, dst, send, recv, device):
        return pltpu.make_async_remote_copy(
            src_ref=src, dst_ref=dst, send_sem=send, recv_sem=recv, device_id=(device,), device_id_type=MESH
        )

    sends = []
    order = list(range(1, planes)) + [0]
    pair = {}
    for d in order:
        q = plane_at(d, 1)
        pair[d] = remote(part.at[1 - core, q], crecv.at[q], c_send.at[d], c_recv.at[d], mate)
        pair[d].start()
    for d in order:
        q = plane_at(d, 1)
        pair[d].wait_recv()
        crecv[q] = crecv[q] + part[core, q]
        if d:
            copy = remote(crecv.at[q], xrecv.at[d], x_send.at[d], x_recv.at[d], plane_device(q))
            copy.start()
            sends.append(copy)
    total = crecv[p]
    for d in range(1, planes):
        sends[d - 1].wait_recv()
        total = total + xrecv[d]
    zflat[...] = total
    for k in range(nz):
        zbuf[k] = zflat[k * zrows:(k + 1) * zrows, :]
    zcopies = []
    for d in range(1, nz):
        k = z_at(d)
        copy = remote(zbuf.at[k], zrecv.at[d], z_send.at[d], z_recv.at[d], z_device(k))
        copy.start()
        zcopies.append(copy)
    mine = zbuf[z]
    for d in range(1, nz):
        zcopies[d - 1].wait_recv()
        mine = mine + zrecv[d]
    zgat[z] = mine
    gcopies = []
    for d in range(1, nz):
        copy = remote(zgat.at[z], zgat.at[z], g_send.at[d], g_recv.at[d], z_device(z_at(d)))
        copy.start()
        gcopies.append(copy)
    for copy in gcopies:
        copy.wait_recv()
    for k in range(nz):
        full[core, p, k * zrows:(k + 1) * zrows, :] = zgat[k]
    acopies = []
    for d in range(1, planes):
        copy = remote(full.at[core, p], full.at[core, p], a_send.at[d], a_recv.at[d], plane_device(plane_at(d, 1)))
        copy.start()
        acopies.append(copy)
    fcopies = []
    for d in range(planes):
        q = plane_at(d, -1)
        if d:
            acopies[d - 1].wait_recv()
        copy = remote(full.at[core, q], full.at[core, q], f_send.at[d], f_recv.at[d], mate)
        copy.start()
        fcopies.append(copy)
    for copy in fcopies:
        copy.wait_recv()
    for copy in [pair[d] for d in order] + sends + zcopies + gcopies + acopies + fcopies:
        copy.wait_send()
    full_out[...] = full[...]


def all_sums(dims, strain, table, seed):
    nx, ny, nz = dims
    planes = nx * ny
    rows = HALF_ROWS // planes
    channels = strain.shape[0]
    vmem = pl.BlockSpec(memory_space=pltpu.VMEM)
    dma = pltpu.SemaphoreType.DMA
    spectrum = jax.ShapeDtypeStruct((SEGMENTS * channels, LINES), jnp.float32)
    return pl.pallas_call(
        functools.partial(sum_kernel, dims),
        out_shape=[jax.ShapeDtypeStruct((2, planes, rows, LINES), jnp.float32), spectrum, spectrum],
        in_specs=[vmem, vmem, pl.BlockSpec(memory_space=pltpu.SMEM)],
        out_specs=[vmem, vmem, vmem],
        scratch_shapes=[
            pltpu.VMEM((2, planes, rows, LINES), jnp.float32),
            pltpu.VMEM((planes, rows, LINES), jnp.float32),
            pltpu.VMEM((planes, rows, LINES), jnp.float32),
            pltpu.VMEM((rows, LINES), jnp.float32),
            pltpu.VMEM((nz, rows // nz, LINES), jnp.float32),
            pltpu.VMEM((nz, rows // nz, LINES), jnp.float32),
            pltpu.VMEM((nz, rows // nz, LINES), jnp.float32),
            pltpu.VMEM((2, planes, rows, LINES), jnp.float32),
        ] + [dma((planes,))] * 4 + [dma((nz,))] * 4 + [dma((planes,))] * 4,
        compiler_params=pltpu.CompilerParams(
            collective_id=0, has_side_effects=True, vmem_limit_bytes=48 * 1024 * 1024
        ),
        name="sums",
    )(strain, table, seed)


def mode_kernel(scaling, root, full, sre, sim, modes, factor, sky, px, py, hx, hy, gram, rows_x, basis):
    channels = sre.shape[0] // SEGMENTS

    def turned(value):
        return jnp.stack([-value[1], value[0]])

    def sketch_of(t):
        row = t * 2 * SKETCH
        return jnp.stack([full[0, row:row + SKETCH, :], full[0, row + SKETCH:row + 2 * SKETCH, :]])

    def gram_of(s, t):
        if s // 8 <= t // 8:
            first, second, sign = t, s, 1
        else:
            first, second, sign = s, t, -1
        row = gram_row(first, second, 0)
        row_im = gram_row(first, second, 1)
        return full[1, row:row + 1, :], full[1, row_im:row_im + 1, :], sign

    for t in range(SEGMENTS):
        sky[t] = turned(sketch_of(t))

    def times_gram(get_x, get_y, out_x, out_y, scale):
        for s0 in range(0, SEGMENTS, 4):
            accs = [jnp.zeros((2, SKETCH, LINES), jnp.float32) for _ in range(4)]
            for t in range(SEGMENTS):
                vx, vy = get_x(t), get_y(t)
                for a in range(4):
                    gre, gim, sign = gram_of(s0 + a, t)
                    if sign > 0:
                        accs[a] = accs[a] + gre * vx + gim * vy
                    else:
                        accs[a] = accs[a] + gre * vx - gim * vy
            for a in range(4):
                value = accs[a] if scale is None else accs[a] * scale * scale
                out_x[s0 + a] = value
                out_y[s0 + a] = turned(value)

    times_gram(sketch_of, lambda t: sky[t], px, py, scaling)
    times_gram(lambda t: px[t], lambda t: py[t], hx, hy, None)

    for j0 in range(0, SKETCH, 4):
        k0 = 8 * (j0 // 8)
        accs = [jnp.zeros((2, SKETCH - k0, LINES), jnp.float32) for _ in range(4)]
        for s in range(SEGMENTS):
            vx, vy = hx[s, :, k0:, :], hy[s, :, k0:, :]
            for a in range(4):
                accs[a] = accs[a] + px[s, 0, j0 + a:j0 + a + 1, :] * vx - px[s, 1, j0 + a:j0 + a + 1, :] * vy
        for a in range(4):
            gram[j0 + a, :, k0:, :] = accs[a]

    for j0 in range(0, SKETCH, 4):
        accs = [jnp.zeros((2, channels, LINES), jnp.float32) for _ in range(4)]
        for s in range(SEGMENTS):
            vx = jnp.stack([sre[s * channels:(s + 1) * channels, :], sim[s * channels:(s + 1) * channels, :]])
            vy = turned(vx)
            for a in range(4):
                accs[a] = accs[a] + px[s, 0, j0 + a:j0 + a + 1, :] * vx + px[s, 1, j0 + a:j0 + a + 1, :] * vy
        for a in range(4):
            basis[j0 + a] = accs[a]

    for i in range(SKETCH):
        k0 = 8 * (i // 8)
        columns = k0 + lax.broadcasted_iota(jnp.int32, (SKETCH - k0, LINES), 0)
        row = gram[i, :, k0:, :]
        diagonal = jnp.sqrt(gram[i, 0, i:i + 1, :])
        inverse = 1.0 / diagonal
        scaled = row * inverse
        re = jnp.where(columns > i, scaled[0], 0.0)
        re = jnp.where(columns == i, diagonal, re)
        im = jnp.where(columns > i, scaled[1], 0.0)
        value = jnp.stack([re, im])
        if k0:
            factor[0, i, :k0, :] = jnp.zeros((k0, LINES), jnp.float32)
            factor[1, i, :k0, :] = jnp.zeros((k0, LINES), jnp.float32)
        factor[0, i, k0:, :] = re
        factor[1, i, k0:, :] = im
        rows_x[i, :, k0:, :] = value
        mode = basis[i] * inverse
        modes[pl.ds(i, channels, stride=2 * SKETCH), :] = mode[0] * root
        modes[pl.ds(i + SKETCH, channels, stride=2 * SKETCH), :] = mode[1] * root
        other = turned(mode)
        for r in range(i + 1, SKETCH):
            r0 = 8 * (r // 8)
            top_re = rows_x[i, 0, r:r + 1, :]
            top_im = rows_x[i, 1, r:r + 1, :]
            late = value[:, r0 - k0:, :]
            gram[r, :, r0:, :] = gram[r, :, r0:, :] - (top_re * late - top_im * turned(late))
            basis[r] = basis[r] - (top_re * mode + top_im * other)


def finish(full, sre, sim, channels_all):
    channels = sre.shape[0] // SEGMENTS
    vmem = pl.BlockSpec(memory_space=pltpu.VMEM)
    kernel = functools.partial(mode_kernel, 1.0 / (SEGMENTS * channels_all), math.sqrt(channels_all))
    tall = pltpu.VMEM((SEGMENTS, 2, SKETCH, LINES), jnp.float32)
    wide = pltpu.VMEM((SKETCH, 2, SKETCH, LINES), jnp.float32)
    return pl.pallas_call(
        kernel,
        out_shape=[
            jax.ShapeDtypeStruct((channels * 2 * SKETCH, LINES), jnp.float32),
            jax.ShapeDtypeStruct((2, SKETCH, SKETCH, LINES), jnp.float32),
        ],
        in_specs=[vmem] * 3,
        out_specs=[vmem] * 2,
        scratch_shapes=[tall] * 5 + [wide] * 2 + [pltpu.VMEM((SKETCH, 2, channels, LINES), jnp.float32)],
        compiler_params=pltpu.CompilerParams(vmem_limit_bytes=48 * 1024 * 1024),
        name="modes",
    )(full, sre, sim)


def shards(dims, strain, band_start, sketch_seed):
    channels, samples = strain.shape
    channels_all = channels * lax.axis_size("ch")
    table = dft_table(band_start, samples // SEGMENTS, LINES)
    full, sre, sim = all_sums(dims, strain, table, sketch_seed)
    modes, factor = finish(full.reshape(2, HALF_ROWS, LINES), sre, sim, channels_all)
    return modes.reshape(channels, 2, SKETCH, LINES), factor


def solution(mesh, dims=(4, 4, 16)):
    in_specs = (P("ch", None), P(), P())
    out_specs = (P("ch", None, None, None), P())
    return jax.shard_map(
        functools.partial(shards, dims), mesh=mesh, in_specs=in_specs, out_specs=out_specs, check_vma=False
    )
```

time: 1560 us -> 59.7 us (0.04)
  waiting for transfers between devices: 1380 us -> 0 us
  local copies, waits for them, and re-layouts: 82 us -> 0.34 us
  Pallas kernels: 0 us -> 56.6 us
  matrix products: 42.7 us -> 0 us
  other arithmetic: 32.8 us -> 0.62 us
    psum x3 -> x0, waiting for transfers between devices: 1380 us -> none  [the longest x1 474 us: shards(): power_re, power_im = lax.psum((power_re, power_im), 'ch')]
    pallas_call x0 -> x2, Pallas kernels: none -> 56.6 us  [the longest x1 51.1 us: all_sums(): pl.pallas_call(functools.partial(sum_kernel, dims), out_shape=[jax.ShapeD...]
    dot_general x25 -> x0, matrix products: 42.7 us -> none  [the longest x24 42.4 us: product(): return jnp.einsum(form, left, right, precision=lax.Precision.HIGHEST)]
    unnamed x330 -> x2, local copies, waits for them, and re-layouts: 41.8 us -> 0.34 us
  transfers between devices with their start and end apart: 3 -> 0, of which waited for: 3 -> 0; matrix products, arithmetic and copies ran while one was open for 1% -> 0% of each run, Pallas kernels for 0% -> 0%
where the time goes in v1:
time: 59.7 us; the launch traced here: 59.5 us
  Pallas kernels  56.6 us (95%)
  between operations  1.96 us (3%)
  other arithmetic  0.62 us (1%)
    pallas_call x1, Pallas kernels, all_sums(): pl.pallas_call(functools.partial(sum_kernel, dims), out_shape=[jax.ShapeD...  51.1 us
    pallas_call x1, Pallas kernels, finish(): pl.pallas_call(kernel, out_shape=[jax.ShapeDtypeStruct((channels * 2 * SK...  5.57 us

profile of v1, /device:TPU:1, one launch (start us, length us, event | category | flops | bytes accessed | tf_op | source)
XLA Modules:
  0.0 59.5 jit_solution(4986849112234373922)
XLA Ops:
  2.0 0.0 copy-start
  2.0 0.6 multiply_convert_fusion.1
  2.6 0.3 copy-done
  2.9 51.1 %sums.1 = (f32[2,16,48,128]{3,2,1,0:T(8,128)S(1)}, f32[384,128]{1,0:T(8,128)S(1)}, f32[384,128]{1,0:T(8,128)S(1)}) custom-call(bf16[16,6144]{1,0:T(8,128)(2,1)S(1)} %copy-done, bf16[256,256]{1,0:T(8,128)(2,1)S(1)} %pad_maximum_fusion.table, s32[1]{0:T(128)S(6)} %copy.6.seed), custom_call_target="tpu_custom_call" | custom-call | tf_op jit(solution)/shard_map/sums/pallas_call | solution.py:212
  54.0 5.6 %modes.1 = (f32[512,128]{1,0:T(8,128)}, f32[2,16,16,128]{3,2,1,0:T(8,128)}) custom-call(f32[2,768,128]{2,1,0:T(8,128)S(1)} %bitcast.4, f32[384,128]{1,0:T(8,128)S(1)} %get-tuple-element.8.sre, f32[384,128]{1,0:T(8,128)S(1)} %get-tuple-element.9.sim), custom_call_target="tpu_custom_call" | custom-call | tf_op jit(solution)/shard_map/modes/pallas_call | solution.py:331
  (3 shorter events, 0.1 us)
Async XLA Ops:
  2.0 0.9 %copy-start = (bf16[16,6144]{1,0:T(8,128)(2,1)S(1)}, bf16[16,6144]{1,0:T(8,128)(2,1)}, u32[]{:S(2)}) copy-start(bf16[16,6144]{1,0:T(8,128)(2,1)} %strain.1) | copy-start | bytes 589828

commit v2 on v1

--- a/solution.py
+++ b/solution.py
@@ -13,6 +13,7 @@
 SKETCH = 16
 HALF_ROWS = SEGMENTS * 2 * SKETCH
 MESH = pl.DeviceIdType.MESH
+GROUP = 4
 
 
 def dft_table(band_start, segment_length, line_count):
@@ -27,20 +28,26 @@
     ).astype(jnp.bfloat16)
 
 
-def sign_block(first_channel, seed, channels, copies):
-    shape = (2 * SKETCH, copies * channels)
+def sign_block(first_channel, seed, channels, copies, group):
+    shape = (group * 2 * SKETCH, group * copies * channels)
     row = lax.broadcasted_iota(jnp.int32, shape, 0)
     col = lax.broadcasted_iota(jnp.int32, shape, 1)
+    inside = jnp.zeros(shape, jnp.bool_)
+    for g in range(group):
+        inside = inside | (
+            (row >= g * 2 * SKETCH) & (row < (g + 1) * 2 * SKETCH)
+            & (col >= g * copies * channels) & (col < (g + 1) * copies * channels)
+        )
     channel = first_channel + jnp.bitwise_and(col, channels - 1)
-    half = (row >= SKETCH).astype(jnp.int32)
-    column = row - half * SKETCH
+    half = jnp.bitwise_and(lax.shift_right_logical(row, jnp.full_like(row, 4)), 1)
+    column = jnp.bitwise_and(row, SKETCH - 1)
     hashed = (channel * SKETCH + column) * 2 + half + seed * 1000003
     hashed = hashed * -1640531535
     hashed = jnp.bitwise_xor(hashed, lax.shift_right_logical(hashed, jnp.full_like(hashed, 15)))
     hashed = hashed * 2146121005
     hashed = jnp.bitwise_xor(hashed, lax.shift_right_logical(hashed, jnp.full_like(hashed, 13)))
     bits = jnp.bitwise_and(lax.shift_right_logical(hashed, jnp.full_like(hashed, 7)), 1)
-    return (1 - 2 * bits).astype(jnp.float32)
+    return jnp.where(inside, (1 - 2 * bits).astype(jnp.float32), 0.0)
 
 
 def gram_row(t, s, part):
@@ -87,73 +94,93 @@
     for d in range(1, nz):
         pl.semaphore_signal(barrier, inc=1, device_id=(z_device(z_at(d)),), device_id_type=MESH)
 
-    for s in range(SEGMENTS):
-        both = jnp.dot(strain[:, s * length:(s + 1) * length], table[...], preferred_element_type=jnp.float32)
-        sre[s * channels:(s + 1) * channels, :] = both[:, :LINES]
-        sim[s * channels:(s + 1) * channels, :] = both[:, LINES:]
-
-    signs = sign_block(me * channels, seed[0], channels, 3).astype(jnp.bfloat16)
-    for s in range(SEGMENTS):
-        both = jnp.concatenate([sre[s * channels:(s + 1) * channels, :], sim[s * channels:(s + 1) * channels, :]], axis=1)
-        high = both.astype(jnp.bfloat16)
-        rest = both - high.astype(jnp.float32)
-        middle = rest.astype(jnp.bfloat16)
-        low = (rest - middle.astype(jnp.float32)).astype(jnp.bfloat16)
-        terms = jnp.concatenate([high, middle, low], axis=0)
-        prod = jnp.dot(signs, terms, preferred_element_type=jnp.float32)
-        for half, value in enumerate((
-            prod[:SKETCH, :LINES] + prod[SKETCH:, LINES:],
-            prod[SKETCH:, :LINES] - prod[:SKETCH, LINES:],
-        )):
-            row = s * 2 * SKETCH + half * SKETCH
-            part[0, row // rows, row % rows:row % rows + SKETCH, :] = value
-
-    for t0 in range(0, SEGMENTS, 4):
+    def remote(src, dst, send, recv, device):
+        return pltpu.make_async_remote_copy(
+            src_ref=src, dst_ref=dst, send_sem=send, recv_sem=recv, device_id=(device,), device_id_type=MESH
+        )
+
+    flat = jnp.concatenate([strain[:, s * length:(s + 1) * length] for s in range(SEGMENTS)], axis=0)
+    both = jnp.dot(flat, table[...], preferred_element_type=jnp.float32)
+    sre[...] = both[:, :LINES]
+    sim[...] = both[:, LINES:]
+
+    signs = sign_block(me * channels, seed[0], channels, 3, GROUP).astype(jnp.bfloat16)
+    for s0 in range(0, SEGMENTS, GROUP):
+        terms = []
+        for s in range(s0, s0 + GROUP):
+            both = jnp.concatenate(
+                [sre[s * channels:(s + 1) * channels, :], sim[s * channels:(s + 1) * channels, :]], axis=1
+            )
+            high = both.astype(jnp.bfloat16)
+            rest = both - high.astype(jnp.float32)
+            middle = rest.astype(jnp.bfloat16)
+            low = (rest - middle.astype(jnp.float32)).astype(jnp.bfloat16)
+            terms += [high, middle, low]
+        prods = jnp.dot(signs, jnp.concatenate(terms, axis=0), preferred_element_type=jnp.float32)
+        for s in range(s0, s0 + GROUP):
+            prod = prods[(s - s0) * 2 * SKETCH:(s - s0 + 1) * 2 * SKETCH, :]
+            for half, value in enumerate((
+                prod[:SKETCH, :LINES] + prod[SKETCH:, LINES:],
+                prod[SKETCH:, :LINES] - prod[:SKETCH, LINES:],
+            )):
+                row = s * 2 * SKETCH + half * SKETCH
+                part[0, row // rows, row % rows:row % rows + SKETCH, :] = value
+
+    pl.semaphore_wait(barrier, planes + nz - 1)
+
+    def pair(half, q):
+        return remote(part.at[half, q], crecv.at[q], c_send.at[q], c_recv.at[q], mate)
+
+    @pl.when(core == 1)
+    def _():
+        for q in range(planes):
+            pair(0, q).start()
+
+    def plane_copy(d):
+        q = plane_at(d, 1)
+        return remote(crecv.at[q], xrecv.at[d], x_send.at[d], x_recv.at[d], plane_device(q))
+
+    def plane_sends():
+        for d in list(range(1, planes)) + [0]:
+            q = plane_at(d, 1)
+            pair(core, q).wait_recv()
+            crecv[q] = crecv[q] + part[core, q]
+            if d:
+                plane_copy(d).start()
+
+    sent = planes
+    for t0 in range(SEGMENTS - 4, -1, -4):
         n = 8 * (t0 // 8 + 1)
-
-        def step(i, accs, t0=t0, n=n):
-            accs = list(accs)
-            for k in range(4):
-                c = i * 4 + k
-                vre = sre[pl.ds(c, n, stride=channels), :]
-                vim = sim[pl.ds(c, n, stride=channels), :]
-                for a in range(4):
-                    bre = sre[pl.ds((t0 + a) * channels + c, 1), :]
-                    bim = sim[pl.ds((t0 + a) * channels + c, 1), :]
-                    accs[2 * a] += vre * bre + vim * bim
-                    accs[2 * a + 1] += vre * bim - vim * bre
-            return tuple(accs)
-
         zero = jnp.zeros((n, LINES), jnp.float32)
-        accs = lax.fori_loop(0, channels // 4, step, (zero,) * 8)
+        accs = [zero] * 8
+        for c in range(channels):
+            vre = sre[pl.ds(c, n, stride=channels), :]
+            vim = sim[pl.ds(c, n, stride=channels), :]
+            for a in range(4):
+                bre = sre[(t0 + a) * channels + c:(t0 + a) * channels + c + 1, :]
+                bim = sim[(t0 + a) * channels + c:(t0 + a) * channels + c + 1, :]
+                accs[2 * a] += vre * bre + vim * bim
+                accs[2 * a + 1] += vre * bim - vim * bre
         for a in range(4):
             for half in range(2):
                 for tile in range(n // 8):
                     row = gram_row(t0 + a, 8 * tile, half)
                     part[1, row // rows, row % rows:row % rows + 8, :] = accs[2 * a + half][8 * tile:8 * tile + 8, :]
-
-    pl.semaphore_wait(barrier, planes + nz - 1)
-
-    def remote(src, dst, send, recv, device):
-        return pltpu.make_async_remote_copy(
-            src_ref=src, dst_ref=dst, send_sem=send, recv_sem=recv, device_id=(device,), device_id_type=MESH
-        )
-
-    sends = []
-    order = list(range(1, planes)) + [0]
-    pair = {}
-    for d in order:
-        q = plane_at(d, 1)
-        pair[d] = remote(part.at[1 - core, q], crecv.at[q], c_send.at[d], c_recv.at[d], mate)
-        pair[d].start()
-    for d in order:
-        q = plane_at(d, 1)
-        pair[d].wait_recv()
-        crecv[q] = crecv[q] + part[core, q]
-        if d:
-            copy = remote(crecv.at[q], xrecv.at[d], x_send.at[d], x_recv.at[d], plane_device(q))
-            copy.start()
-            sends.append(copy)
+        ready = [q for q in range(sent) if q * rows >= gram_row(t0, 0, 0)]
+        sent -= len(ready)
+
+        @pl.when(core == 0)
+        def _(ready=ready, t0=t0):
+            for q in ready:
+                pair(1, q).start()
+            if t0 == 8:
+                plane_sends()
+
+    @pl.when(core == 1)
+    def _():
+        plane_sends()
+
+    sends = [plane_copy(d) for d in range(1, planes)]
     total = crecv[p]
     for d in range(1, planes):
         sends[d - 1].wait_recv()
@@ -196,7 +223,7 @@
         fcopies.append(copy)
     for copy in fcopies:
         copy.wait_recv()
-    for copy in [pair[d] for d in order] + sends + zcopies + gcopies + acopies + fcopies:
+    for copy in [pair(1 - core, q) for q in range(planes)] + sends + zcopies + gcopies + acopies + fcopies:
         copy.wait_send()
     full_out[...] = full[...]
 

time: 59.7 us -> 60.4 us (1.012)
  Pallas kernels: 56.6 us -> 57.3 us
    pallas_call x1, Pallas kernels: 51.1 us -> 51.7 us  [all_sums(): pl.pallas_call(functools.partial(sum_kernel, dims), out_shape=[jax.ShapeD...]
where the time goes in v2:
time: 60.4 us; the launch traced here: 60.2 us
  Pallas kernels  57.3 us (95%)
  between operations  1.96 us (3%)
  other arithmetic  0.62 us (1%)
    pallas_call x1, Pallas kernels, all_sums(): pl.pallas_call(functools.partial(sum_kernel, dims), out_shape=[jax.ShapeD...  51.7 us
    pallas_call x1, Pallas kernels, finish(): pl.pallas_call(kernel, out_shape=[jax.ShapeDtypeStruct((channels * 2 * SK...  5.57 us

profile of v2, /device:TPU:1, one launch (start us, length us, event | category | flops | bytes accessed | tf_op | source)
XLA Modules:
  0.0 60.2 jit_solution(10933770789570893642)
XLA Ops:
  2.0 0.0 copy-start
  2.0 0.6 multiply_convert_fusion.1
  2.6 0.3 copy-done
  2.9 51.7 %sums.1 = (f32[2,16,48,128]{3,2,1,0:T(8,128)S(1)}, f32[384,128]{1,0:T(8,128)S(1)}, f32[384,128]{1,0:T(8,128)S(1)}) custom-call(bf16[16,6144]{1,0:T(8,128)(2,1)S(1)} %copy-done, bf16[256,256]{1,0:T(8,128)(2,1)S(1)} %pad_maximum_fusion.table, s32[1]{0:T(128)S(6)} %copy.6.seed), custom_call_target="tpu_custom_call" | custom-call | tf_op jit(solution)/shard_map/sums/pallas_call | solution.py:239
  54.7 5.6 %modes.1 = (f32[512,128]{1,0:T(8,128)}, f32[2,16,16,128]{3,2,1,0:T(8,128)}) custom-call(f32[2,768,128]{2,1,0:T(8,128)S(1)} %bitcast.4, f32[384,128]{1,0:T(8,128)S(1)} %get-tuple-element.8.sre, f32[384,128]{1,0:T(8,128)S(1)} %get-tuple-element.9.sim), custom_call_target="tpu_custom_call" | custom-call | tf_op jit(solution)/shard_map/modes/pallas_call | solution.py:358
  (3 shorter events, 0.1 us)
Async XLA Ops:
  2.0 0.9 %copy-start = (bf16[16,6144]{1,0:T(8,128)(2,1)S(1)}, bf16[16,6144]{1,0:T(8,128)(2,1)}, u32[]{:S(2)}) copy-start(bf16[16,6144]{1,0:T(8,128)(2,1)} %strain.1) | copy-start | bytes 589828

commit v3 on v2

--- a/solution.py
+++ b/solution.py
@@ -128,25 +128,16 @@
 
     pl.semaphore_wait(barrier, planes + nz - 1)
 
-    def pair(half, q):
-        return remote(part.at[half, q], crecv.at[q], c_send.at[q], c_recv.at[q], mate)
+    def landed(ref, sem):
+        pltpu.make_async_copy(ref, ref, sem).wait()
+
+    def pair(half, q, count):
+        span = pl.ds(q, count)
+        return remote(part.at[half, span], crecv.at[span], c_send, c_recv, mate)
 
     @pl.when(core == 1)
     def _():
-        for q in range(planes):
-            pair(0, q).start()
-
-    def plane_copy(d):
-        q = plane_at(d, 1)
-        return remote(crecv.at[q], xrecv.at[d], x_send.at[d], x_recv.at[d], plane_device(q))
-
-    def plane_sends():
-        for d in list(range(1, planes)) + [0]:
-            q = plane_at(d, 1)
-            pair(core, q).wait_recv()
-            crecv[q] = crecv[q] + part[core, q]
-            if d:
-                plane_copy(d).start()
+        pair(0, 0, planes).start()
 
     sent = planes
     for t0 in range(SEGMENTS - 4, -1, -4):
@@ -166,24 +157,22 @@
                 for tile in range(n // 8):
                     row = gram_row(t0 + a, 8 * tile, half)
                     part[1, row // rows, row % rows:row % rows + 8, :] = accs[2 * a + half][8 * tile:8 * tile + 8, :]
-        ready = [q for q in range(sent) if q * rows >= gram_row(t0, 0, 0)]
-        sent -= len(ready)
-
-        @pl.when(core == 0)
-        def _(ready=ready, t0=t0):
-            for q in ready:
-                pair(1, q).start()
-            if t0 == 8:
-                plane_sends()
-
-    @pl.when(core == 1)
-    def _():
-        plane_sends()
-
-    sends = [plane_copy(d) for d in range(1, planes)]
-    total = crecv[p]
+        first = -(-gram_row(t0, 0, 0) // rows)
+
+        if first < sent:
+            @pl.when(core == 0)
+            def _(first=first, count=sent - first):
+                pair(1, first, count).start()
+        sent = min(sent, first)
+
+    landed(crecv, c_recv)
     for d in range(1, planes):
-        sends[d - 1].wait_recv()
+        q = plane_at(d, 1)
+        crecv[q] = crecv[q] + part[core, q]
+        remote(crecv.at[q], xrecv.at[d], x_send, x_recv, plane_device(q)).start()
+    total = crecv[p] + part[core, p]
+    landed(xrecv.at[pl.ds(1, planes - 1)], x_recv)
+    for d in range(1, planes):
         total = total + xrecv[d]
     zflat[...] = total
     for k in range(nz):
@@ -210,20 +199,20 @@
         full[core, p, k * zrows:(k + 1) * zrows, :] = zgat[k]
     acopies = []
     for d in range(1, planes):
-        copy = remote(full.at[core, p], full.at[core, p], a_send.at[d], a_recv.at[d], plane_device(plane_at(d, 1)))
+        copy = remote(full.at[core, p], full.at[core, p], a_send, a_recv.at[d], plane_device(plane_at(d, 1)))
         copy.start()
         acopies.append(copy)
-    fcopies = []
     for d in range(planes):
         q = plane_at(d, -1)
         if d:
             acopies[d - 1].wait_recv()
-        copy = remote(full.at[core, q], full.at[core, q], f_send.at[d], f_recv.at[d], mate)
-        copy.start()
-        fcopies.append(copy)
-    for copy in fcopies:
-        copy.wait_recv()
-    for copy in [pair(1 - core, q) for q in range(planes)] + sends + zcopies + gcopies + acopies + fcopies:
+        remote(full.at[core, q], full.at[core, q], f_send, f_recv, mate).start()
+    landed(full.at[1 - core], f_recv)
+    landed(full.at[core], f_send)
+    landed(crecv, c_send)
+    landed(xrecv.at[pl.ds(1, planes - 1)], x_send)
+    landed(xrecv.at[pl.ds(1, planes - 1)], a_send)
+    for copy in zcopies + gcopies:
         copy.wait_send()
     full_out[...] = full[...]
 
@@ -250,7 +239,7 @@
             pltpu.VMEM((nz, rows // nz, LINES), jnp.float32),
             pltpu.VMEM((nz, rows // nz, LINES), jnp.float32),
             pltpu.VMEM((2, planes, rows, LINES), jnp.float32),
-        ] + [dma((planes,))] * 4 + [dma((nz,))] * 4 + [dma((planes,))] * 4,
+        ] + [dma(())] * 4 + [dma((nz,))] * 4 + [dma(()), dma((planes,)), dma(()), dma(())],
         compiler_params=pltpu.CompilerParams(
             collective_id=0, has_side_effects=True, vmem_limit_bytes=48 * 1024 * 1024
         ),

time: 60.4 us -> 59.3 us (0.982)
  Pallas kernels: 57.3 us -> 56.2 us
    pallas_call x1, Pallas kernels: 51.7 us -> 50.7 us  [all_sums(): pl.pallas_call(functools.partial(sum_kernel, dims), out_shape=[jax.ShapeD...]
where the time goes in v3:
time: 59.3 us; the launch traced here: 59.2 us
  Pallas kernels  56.2 us (95%)
  between operations  1.96 us (3%)
  other arithmetic  0.62 us (1%)
    pallas_call x1, Pallas kernels, all_sums(): pl.pallas_call(functools.partial(sum_kernel, dims), out_shape=[jax.ShapeD...  50.7 us
    pallas_call x1, Pallas kernels, finish(): pl.pallas_call(kernel, out_shape=[jax.ShapeDtypeStruct((channels * 2 * SK...  5.57 us

profile of v3, /device:TPU:1, one launch (start us, length us, event | category | flops | bytes accessed | tf_op | source)
XLA Modules:
  0.0 59.2 jit_solution(6034925636223527329)
XLA Ops:
  2.0 0.0 copy-start
  2.0 0.6 multiply_convert_fusion.1
  2.6 0.3 copy-done
  2.9 50.7 %sums.1 = (f32[2,16,48,128]{3,2,1,0:T(8,128)S(1)}, f32[384,128]{1,0:T(8,128)S(1)}, f32[384,128]{1,0:T(8,128)S(1)}) custom-call(bf16[16,6144]{1,0:T(8,128)(2,1)S(1)} %copy-done, bf16[256,256]{1,0:T(8,128)(2,1)S(1)} %pad_maximum_fusion.table, s32[1]{0:T(128)S(6)} %copy.6.seed), custom_call_target="tpu_custom_call" | custom-call | tf_op jit(solution)/shard_map/sums/pallas_call | solution.py:228
  53.6 5.6 %modes.1 = (f32[512,128]{1,0:T(8,128)}, f32[2,16,16,128]{3,2,1,0:T(8,128)}) custom-call(f32[2,768,128]{2,1,0:T(8,128)S(1)} %bitcast.4, f32[384,128]{1,0:T(8,128)S(1)} %get-tuple-element.8.sre, f32[384,128]{1,0:T(8,128)S(1)} %get-tuple-element.9.sim), custom_call_target="tpu_custom_call" | custom-call | tf_op jit(solution)/shard_map/modes/pallas_call | solution.py:347
  (3 shorter events, 0.1 us)
Async XLA Ops:
  2.0 0.9 %copy-start = (bf16[16,6144]{1,0:T(8,128)(2,1)S(1)}, bf16[16,6144]{1,0:T(8,128)(2,1)}, u32[]{:S(2)}) copy-start(bf16[16,6144]{1,0:T(8,128)(2,1)} %strain.1) | copy-start | bytes 589828

commit v4 on v3

--- a/solution.py
+++ b/solution.py
@@ -56,12 +56,11 @@
 
 
 def sum_kernel(dims, strain, table, seed, full_out, sre, sim,
-               part, crecv, xrecv, zflat, zbuf, zrecv, zgat, full,
-               c_send, c_recv, x_send, x_recv, z_send, z_recv, g_send, g_recv, a_send, a_recv, f_send, f_recv):
+               part, crecv, xrecv, zall, full,
+               c_send, c_recv, x_send, x_recv, z_send, z_recv, a_send, a_recv, f_send, f_recv):
     nx, ny, nz = dims
-    planes = nx * ny
-    rows = HALF_ROWS // planes
-    zrows = rows // nz
+    units = nx * ny * 2
+    rows = HALF_ROWS // units
     channels = strain.shape[0]
     length = table.shape[0]
 
@@ -70,29 +69,38 @@
     z = lax.rem(lax.div(me, 2), nz)
     p = lax.div(me, 2 * nz)
     x, y = lax.div(p, ny), lax.rem(p, ny)
+    odd, level = lax.rem(z, 2), lax.div(z, 2)
     mate = me + 1 - 2 * core
-
-    def plane_at(d, sign):
-        dx, dy = d // ny, d % ny
+    here = p * 2 + odd
+
+    def unit_at(d, sign):
+        dx, dy, flip = d // 2 // ny, d // 2 % ny, d % 2
         qx = lax.rem(x + (dx if sign > 0 else nx - dx), nx)
         qy = lax.rem(y + (dy if sign > 0 else ny - dy), ny)
-        return qx * ny + qy
-
-    def plane_device(q):
-        return q * (2 * nz) + z * 2 + core
-
-    def z_at(d):
-        return lax.rem(z + d, nz)
-
-    def z_device(k):
-        return p * (2 * nz) + k * 2 + core
+        return (qx * ny + qy) * 2 + (1 - odd if flip else odd)
+
+    def hops(d):
+        dx, dy = d // 2 // ny, d // 2 % ny
+        return min(dx, nx - dx) + min(dy, ny - dy) + d % 2
+
+    far_first = sorted(range(1, units), key=lambda d: (-hops(d), d))
+
+    def unit_device(u):
+        return lax.div(u, 2) * (2 * nz) + (level * 2 + lax.rem(u, 2)) * 2 + core
+
+    def level_device(e):
+        return p * (2 * nz) + (lax.rem(level + e, nz // 2) * 2 + odd) * 2 + core
 
     barrier = pltpu.get_barrier_semaphore()
+    for e in range(1, nz // 2):
+        pl.semaphore_signal(barrier, inc=1, device_id=(level_device(e),), device_id_type=MESH)
+    for d in far_first:
+        pl.semaphore_signal(barrier, inc=1, device_id=(unit_device(unit_at(d, 1)),), device_id_type=MESH)
     pl.semaphore_signal(barrier, inc=1, device_id=(mate,), device_id_type=MESH)
-    for d in range(1, planes):
-        pl.semaphore_signal(barrier, inc=1, device_id=(plane_device(plane_at(d, 1)),), device_id_type=MESH)
-    for d in range(1, nz):
-        pl.semaphore_signal(barrier, inc=1, device_id=(z_device(z_at(d)),), device_id_type=MESH)
+
+    def put(half, row, value):
+        for r in range(row, row + value.shape[0], 8):
+            part[half, r // rows, r % rows:r % rows + 8, :] = value[r - row:r - row + 8, :]
 
     def remote(src, dst, send, recv, device):
         return pltpu.make_async_remote_copy(
@@ -124,9 +132,9 @@
                 prod[SKETCH:, :LINES] - prod[:SKETCH, LINES:],
             )):
                 row = s * 2 * SKETCH + half * SKETCH
-                part[0, row // rows, row % rows:row % rows + SKETCH, :] = value
-
-    pl.semaphore_wait(barrier, planes + nz - 1)
+                put(0, row, value)
+
+    pl.semaphore_wait(barrier, units + nz // 2 - 1)
 
     def landed(ref, sem):
         pltpu.make_async_copy(ref, ref, sem).wait()
@@ -137,9 +145,9 @@
 
     @pl.when(core == 1)
     def _():
-        pair(0, 0, planes).start()
-
-    sent = planes
+        pair(0, 0, units).start()
+
+    sent = units
     for t0 in range(SEGMENTS - 4, -1, -4):
         n = 8 * (t0 // 8 + 1)
         zero = jnp.zeros((n, LINES), jnp.float32)
@@ -156,7 +164,7 @@
             for half in range(2):
                 for tile in range(n // 8):
                     row = gram_row(t0 + a, 8 * tile, half)
-                    part[1, row // rows, row % rows:row % rows + 8, :] = accs[2 * a + half][8 * tile:8 * tile + 8, :]
+                    put(1, row, accs[2 * a + half][8 * tile:8 * tile + 8, :])
         first = -(-gram_row(t0, 0, 0) // rows)
 
         if first < sent:
@@ -166,80 +174,58 @@
         sent = min(sent, first)
 
     landed(crecv, c_recv)
-    for d in range(1, planes):
-        q = plane_at(d, 1)
-        crecv[q] = crecv[q] + part[core, q]
-        remote(crecv.at[q], xrecv.at[d], x_send, x_recv, plane_device(q)).start()
-    total = crecv[p] + part[core, p]
-    landed(xrecv.at[pl.ds(1, planes - 1)], x_recv)
-    for d in range(1, planes):
+    for d in far_first:
+        u = unit_at(d, 1)
+        crecv[u] = crecv[u] + part[core, u]
+        remote(crecv.at[u], xrecv.at[d], x_send, x_recv, unit_device(u)).start()
+    total = crecv[here] + part[core, here]
+    landed(xrecv.at[pl.ds(1, units - 1)], x_recv)
+    for d in range(1, units):
         total = total + xrecv[d]
-    zflat[...] = total
-    for k in range(nz):
-        zbuf[k] = zflat[k * zrows:(k + 1) * zrows, :]
-    zcopies = []
-    for d in range(1, nz):
-        k = z_at(d)
-        copy = remote(zbuf.at[k], zrecv.at[d], z_send.at[d], z_recv.at[d], z_device(k))
-        copy.start()
-        zcopies.append(copy)
-    mine = zbuf[z]
-    for d in range(1, nz):
-        zcopies[d - 1].wait_recv()
-        mine = mine + zrecv[d]
-    zgat[z] = mine
-    gcopies = []
-    for d in range(1, nz):
-        copy = remote(zgat.at[z], zgat.at[z], g_send.at[d], g_recv.at[d], z_device(z_at(d)))
-        copy.start()
-        gcopies.append(copy)
-    for copy in gcopies:
-        copy.wait_recv()
-    for k in range(nz):
-        full[core, p, k * zrows:(k + 1) * zrows, :] = zgat[k]
-    acopies = []
-    for d in range(1, planes):
-        copy = remote(full.at[core, p], full.at[core, p], a_send, a_recv.at[d], plane_device(plane_at(d, 1)))
-        copy.start()
-        acopies.append(copy)
-    for d in range(planes):
-        q = plane_at(d, -1)
+    zall[level] = total
+    for e in range(1, nz // 2):
+        remote(zall.at[level], zall.at[level], z_send, z_recv, level_device(e)).start()
+    landed(zall.at[pl.ds(1, nz // 2 - 1)], z_recv)
+    total = zall[0]
+    for e in range(1, nz // 2):
+        total = total + zall[e]
+    full[core, here] = total
+    for d in far_first:
+        remote(full.at[core, here], full.at[core, here], a_send, a_recv.at[d], unit_device(unit_at(d, 1))).start()
+    for d in [0] + far_first:
+        u = unit_at(d, -1)
         if d:
-            acopies[d - 1].wait_recv()
-        remote(full.at[core, q], full.at[core, q], f_send, f_recv, mate).start()
+            remote(full.at[core, u], full.at[core, u], a_send, a_recv.at[d], unit_device(u)).wait_recv()
+        remote(full.at[core, u], full.at[core, u], f_send, f_recv, mate).start()
     landed(full.at[1 - core], f_recv)
     landed(full.at[core], f_send)
     landed(crecv, c_send)
-    landed(xrecv.at[pl.ds(1, planes - 1)], x_send)
-    landed(xrecv.at[pl.ds(1, planes - 1)], a_send)
-    for copy in zcopies + gcopies:
-        copy.wait_send()
+    landed(zall.at[pl.ds(1, nz // 2 - 1)], z_send)
+    landed(xrecv.at[pl.ds(1, units - 1)], x_send)
+    landed(xrecv.at[pl.ds(1, units - 1)], a_send)
     full_out[...] = full[...]
 
 
 def all_sums(dims, strain, table, seed):
     nx, ny, nz = dims
-    planes = nx * ny
-    rows = HALF_ROWS // planes
+    units = nx * ny * 2
+    rows = HALF_ROWS // units
     channels = strain.shape[0]
     vmem = pl.BlockSpec(memory_space=pltpu.VMEM)
     dma = pltpu.SemaphoreType.DMA
     spectrum = jax.ShapeDtypeStruct((SEGMENTS * channels, LINES), jnp.float32)
     return pl.pallas_call(
         functools.partial(sum_kernel, dims),
-        out_shape=[jax.ShapeDtypeStruct((2, planes, rows, LINES), jnp.float32), spectrum, spectrum],
+        out_shape=[jax.ShapeDtypeStruct((2, units, rows, LINES), jnp.float32), spectrum, spectrum],
         in_specs=[vmem, vmem, pl.BlockSpec(memory_space=pltpu.SMEM)],
         out_specs=[vmem, vmem, vmem],
         scratch_shapes=[
-            pltpu.VMEM((2, planes, rows, LINES), jnp.float32),
-            pltpu.VMEM((planes, rows, LINES), jnp.float32),
-            pltpu.VMEM((planes, rows, LINES), jnp.float32),
-            pltpu.VMEM((rows, LINES), jnp.float32),
-            pltpu.VMEM((nz, rows // nz, LINES), jnp.float32),
-            pltpu.VMEM((nz, rows // nz, LINES), jnp.float32),
-            pltpu.VMEM((nz, rows // nz, LINES), jnp.float32),
-            pltpu.VMEM((2, planes, rows, LINES), jnp.float32),
-        ] + [dma(())] * 4 + [dma((nz,))] * 4 + [dma(()), dma((planes,)), dma(()), dma(())],
+            pltpu.VMEM((2, units, rows, LINES), jnp.float32),
+            pltpu.VMEM((units, rows, LINES), jnp.float32),
+            pltpu.VMEM((units, rows, LINES), jnp.float32),
+            pltpu.VMEM((nz // 2, rows, LINES), jnp.float32),
+            pltpu.VMEM((2, units, rows, LINES), jnp.float32),
+        ] + [dma(())] * 7 + [dma((units,)), dma(()), dma(())],
         compiler_params=pltpu.CompilerParams(
             collective_id=0, has_side_effects=True, vmem_limit_bytes=48 * 1024 * 1024
         ),

time: 59.3 us -> 51.5 us (0.87)
  Pallas kernels: 56.2 us -> 48.4 us
    pallas_call x1, Pallas kernels: 50.7 us -> 42.9 us  [all_sums(): pl.pallas_call(functools.partial(sum_kernel, dims), out_shape=[jax.ShapeD...]
where the time goes in v4:
time: 51.5 us; the launch traced here: 51.4 us
  Pallas kernels  48.4 us (94%)
  between operations  1.96 us (4%)
  other arithmetic  0.62 us (1%)
    pallas_call x1, Pallas kernels, all_sums(): pl.pallas_call(functools.partial(sum_kernel, dims), out_shape=[jax.ShapeD...  42.9 us
    pallas_call x1, Pallas kernels, finish(): pl.pallas_call(kernel, out_shape=[jax.ShapeDtypeStruct((channels * 2 * SK...  5.57 us

profile of v4, /device:TPU:1, one launch (start us, length us, event | category | flops | bytes accessed | tf_op | source)
XLA Modules:
  0.0 51.4 jit_solution(13367536366487327530)
XLA Ops:
  2.0 0.0 copy-start
  2.0 0.6 %multiply_convert_fusion.1 = (bf16[256,128]{1,0:T(8,128)(2,1)S(1)}, bf16[256,128]{1,0:T(8,128)(2,1)S(1)}) fusion(s32[128]{0:T(128)S(1)} %iota_add_fusion, f32[256]{0:T(256)S(1)} %get-tuple-element.14, f32[256]{0:T(256)S(1)} %get-tuple-element.15), kind=kLoop, calls=%fused_computation.8 | loop fusion | flops 589824 | bytes 133632 | tf_op jit(solution)/shard_map/convert
  2.6 0.3 copy-done
  2.9 42.9 %sums.1 = (f32[2,32,24,128]{3,2,1,0:T(8,128)S(1)}, f32[384,128]{1,0:T(8,128)S(1)}, f32[384,128]{1,0:T(8,128)S(1)}) custom-call(bf16[16,6144]{1,0:T(8,128)(2,1)S(1)} %copy-done, bf16[256,256]{1,0:T(8,128)(2,1)S(1)} %pad_maximum_fusion.table, s32[1]{0:T(128)S(6)} %copy.6.seed), custom_call_target="tpu_custom_call" | custom-call | tf_op jit(solution)/shard_map/sums/pallas_call | solution.py:217
  45.8 5.6 %modes.1 = (f32[512,128]{1,0:T(8,128)}, f32[2,16,16,128]{3,2,1,0:T(8,128)}) custom-call(f32[2,768,128]{2,1,0:T(8,128)S(1)} %bitcast.4, f32[384,128]{1,0:T(8,128)S(1)} %get-tuple-element.8.sre, f32[384,128]{1,0:T(8,128)S(1)} %get-tuple-element.9.sim), custom_call_target="tpu_custom_call" | custom-call | tf_op jit(solution)/shard_map/modes/pallas_call | solution.py:333
  (3 shorter events, 0.1 us)
Async XLA Ops:
  2.0 0.9 %copy-start = (bf16[16,6144]{1,0:T(8,128)(2,1)S(1)}, bf16[16,6144]{1,0:T(8,128)(2,1)}, u32[]{:S(2)}) copy-start(bf16[16,6144]{1,0:T(8,128)(2,1)} %strain.1) | copy-start | bytes 589828

commit v5 on v4

--- a/solution.py
+++ b/solution.py
@@ -233,66 +233,105 @@
     )(strain, table, seed)
 
 
-def mode_kernel(scaling, root, full, sre, sim, modes, factor, sky, px, py, hx, hy, gram, rows_x, basis):
+def mode_kernel(scaling, root, full, sre, sim, modes, factor, gsum, sksum, px, psum, pdiff, hx, hsum, ssum, gram, rows_x, basis):
     channels = sre.shape[0] // SEGMENTS
 
     def turned(value):
         return jnp.stack([-value[1], value[0]])
 
+    for t in range(SEGMENTS):
+        n = 8 * (t // 8 + 1)
+        re = full[1, gram_row(t, 0, 0):gram_row(t, 0, 0) + n, :]
+        im = full[1, gram_row(t, 0, 1):gram_row(t, 0, 1) + n, :]
+        gsum[0, t, :n, :] = re + im
+        gsum[1, t, :n, :] = re - im
+    for t in range(SEGMENTS):
+        row = t * 2 * SKETCH
+        sksum[t] = full[0, row:row + SKETCH, :] + full[0, row + SKETCH:row + 2 * SKETCH, :]
+
     def sketch_of(t):
         row = t * 2 * SKETCH
-        return jnp.stack([full[0, row:row + SKETCH, :], full[0, row + SKETCH:row + 2 * SKETCH, :]])
+        return full[0, row:row + SKETCH, :], full[0, row + SKETCH:row + 2 * SKETCH, :], sksum[t]
 
     def gram_of(s, t):
-        if s // 8 <= t // 8:
-            first, second, sign = t, s, 1
-        else:
-            first, second, sign = s, t, -1
+        sign = s // 8 <= t // 8
+        first, second = (t, s) if sign else (s, t)
         row = gram_row(first, second, 0)
         row_im = gram_row(first, second, 1)
-        return full[1, row:row + 1, :], full[1, row_im:row_im + 1, :], sign
-
-    for t in range(SEGMENTS):
-        sky[t] = turned(sketch_of(t))
-
-    def times_gram(get_x, get_y, out_x, out_y, scale):
+        third = gsum[0 if sign else 1, first, second:second + 1, :]
+        return full[1, row:row + 1, :], full[1, row_im:row_im + 1, :], third, sign
+
+    def sums(count, shape, left, right):
+        accs = [[jnp.zeros(shape, jnp.float32) for _ in range(4)] for _ in range(count)]
+        kinds = [set() for _ in range(count)]
+        for s in range(SEGMENTS):
+            vre, vim, vsum = right(s)
+            for a in range(count):
+                lre, lim, third, straight = left(s, a)
+                kinds[a].add(straight)
+                accs[a][0] = accs[a][0] + lre * vre
+                if straight:
+                    accs[a][1] = accs[a][1] + lim * vim
+                else:
+                    accs[a][2] = accs[a][2] + lim * vim
+                accs[a][3] = accs[a][3] + third * vsum
+        out = []
+        for a in range(count):
+            prod_re, straight, conjugate, both = accs[a]
+            im = both - prod_re
+            re = prod_re
+            if True in kinds[a]:
+                im, re = im - straight, re - straight
+            if False in kinds[a]:
+                im, re = im + conjugate, re + conjugate
+            out.append((re, im))
+        return out
+
+    def times_gram(right, scale, store):
         for s0 in range(0, SEGMENTS, 4):
-            accs = [jnp.zeros((2, SKETCH, LINES), jnp.float32) for _ in range(4)]
-            for t in range(SEGMENTS):
-                vx, vy = get_x(t), get_y(t)
-                for a in range(4):
-                    gre, gim, sign = gram_of(s0 + a, t)
-                    if sign > 0:
-                        accs[a] = accs[a] + gre * vx + gim * vy
-                    else:
-                        accs[a] = accs[a] + gre * vx - gim * vy
-            for a in range(4):
-                value = accs[a] if scale is None else accs[a] * scale * scale
-                out_x[s0 + a] = value
-                out_y[s0 + a] = turned(value)
-
-    times_gram(sketch_of, lambda t: sky[t], px, py, scaling)
-    times_gram(lambda t: px[t], lambda t: py[t], hx, hy, None)
+            for a, (re, im) in enumerate(sums(4, (SKETCH, LINES), lambda t, a: gram_of(s0 + a, t), right)):
+                store(s0 + a, re if scale is None else re * scale * scale, im if scale is None else im * scale * scale)
+
+    def store_p(s, re, im):
+        px[s, 0] = re
+        px[s, 1] = im
+        psum[s] = re + im
+        pdiff[s] = re - im
+
+    def store_h(s, re, im):
+        hx[s, 0] = re
+        hx[s, 1] = im
+        hsum[s] = re + im
+
+    times_gram(sketch_of, scaling, store_p)
+    times_gram(lambda t: (px[t, 0], px[t, 1], psum[t]), None, store_h)
 
     for j0 in range(0, SKETCH, 4):
         k0 = 8 * (j0 // 8)
-        accs = [jnp.zeros((2, SKETCH - k0, LINES), jnp.float32) for _ in range(4)]
-        for s in range(SEGMENTS):
-            vx, vy = hx[s, :, k0:, :], hy[s, :, k0:, :]
-            for a in range(4):
-                accs[a] = accs[a] + px[s, 0, j0 + a:j0 + a + 1, :] * vx - px[s, 1, j0 + a:j0 + a + 1, :] * vy
-        for a in range(4):
-            gram[j0 + a, :, k0:, :] = accs[a]
-
+
+        def left(s, a):
+            j = j0 + a
+            return px[s, 0, j:j + 1, :], px[s, 1, j:j + 1, :], pdiff[s, j:j + 1, :], False
+
+        right = lambda s: (hx[s, 0, k0:, :], hx[s, 1, k0:, :], hsum[s, k0:, :])
+        for a, (re, im) in enumerate(sums(4, (SKETCH - k0, LINES), left, right)):
+            gram[j0 + a, 0, k0:, :] = re
+            gram[j0 + a, 1, k0:, :] = im
+
+    ssum[...] = sre[...] + sim[...]
     for j0 in range(0, SKETCH, 4):
-        accs = [jnp.zeros((2, channels, LINES), jnp.float32) for _ in range(4)]
-        for s in range(SEGMENTS):
-            vx = jnp.stack([sre[s * channels:(s + 1) * channels, :], sim[s * channels:(s + 1) * channels, :]])
-            vy = turned(vx)
-            for a in range(4):
-                accs[a] = accs[a] + px[s, 0, j0 + a:j0 + a + 1, :] * vx + px[s, 1, j0 + a:j0 + a + 1, :] * vy
-        for a in range(4):
-            basis[j0 + a] = accs[a]
+
+        def left(s, a):
+            j = j0 + a
+            return px[s, 0, j:j + 1, :], px[s, 1, j:j + 1, :], psum[s, j:j + 1, :], True
+
+        def right(s):
+            span = slice(s * channels, (s + 1) * channels)
+            return sre[span, :], sim[span, :], ssum[span, :]
+
+        for a, (re, im) in enumerate(sums(4, (channels, LINES), left, right)):
+            basis[j0 + a, 0] = re
+            basis[j0 + a, 1] = im
 
     for i in range(SKETCH):
         k0 = 8 * (i // 8)
@@ -329,6 +368,7 @@
     vmem = pl.BlockSpec(memory_space=pltpu.VMEM)
     kernel = functools.partial(mode_kernel, 1.0 / (SEGMENTS * channels_all), math.sqrt(channels_all))
     tall = pltpu.VMEM((SEGMENTS, 2, SKETCH, LINES), jnp.float32)
+    short = pltpu.VMEM((SEGMENTS, SKETCH, LINES), jnp.float32)
     wide = pltpu.VMEM((SKETCH, 2, SKETCH, LINES), jnp.float32)
     return pl.pallas_call(
         kernel,
@@ -338,7 +378,11 @@
         ],
         in_specs=[vmem] * 3,
         out_specs=[vmem] * 2,
-        scratch_shapes=[tall] * 5 + [wide] * 2 + [pltpu.VMEM((SKETCH, 2, channels, LINES), jnp.float32)],
+        scratch_shapes=[
+            pltpu.VMEM((2, SEGMENTS, SEGMENTS, LINES), jnp.float32), short, tall, short, short, tall, short,
+            pltpu.VMEM((SEGMENTS * channels, LINES), jnp.float32),
+            wide, wide, pltpu.VMEM((SKETCH, 2, channels, LINES), jnp.float32),
+        ],
         compiler_params=pltpu.CompilerParams(vmem_limit_bytes=48 * 1024 * 1024),
         name="modes",
     )(full, sre, sim)

time: 51.5 us -> 50.7 us (0.984)
  Pallas kernels: 48.4 us -> 47.6 us
    pallas_call x1, Pallas kernels: 5.57 us -> 4.73 us  [finish(): pl.pallas_call(kernel, out_shape=[jax.ShapeDtypeStruct((channels * 2 * SK...]
where the time goes in v5:
time: 50.7 us; the launch traced here: 50.5 us
  Pallas kernels  47.6 us (94%)
  between operations  1.96 us (4%)
  other arithmetic  0.62 us (1%)
    pallas_call x1, Pallas kernels, all_sums(): pl.pallas_call(functools.partial(sum_kernel, dims), out_shape=[jax.ShapeD...  42.9 us
    pallas_call x1, Pallas kernels, finish(): pl.pallas_call(kernel, out_shape=[jax.ShapeDtypeStruct((channels * 2 * SK...  4.73 us

profile of v5, /device:TPU:1, one launch (start us, length us, event | category | flops | bytes accessed | tf_op | source)
XLA Modules:
  0.0 50.5 jit_solution(151250133667442517)
XLA Ops:
  2.0 0.0 copy-start
  2.0 0.6 %multiply_convert_fusion.1 = (bf16[256,128]{1,0:T(8,128)(2,1)S(1)}, bf16[256,128]{1,0:T(8,128)(2,1)S(1)}) fusion(s32[128]{0:T(128)S(1)} %iota_add_fusion, f32[256]{0:T(256)S(1)} %get-tuple-element.14, f32[256]{0:T(256)S(1)} %get-tuple-element.15), kind=kLoop, calls=%fused_computation.8 | loop fusion | flops 589824 | bytes 133632 | tf_op jit(solution)/shard_map/convert
  2.6 0.3 copy-done
  2.9 42.9 %sums.1 = (f32[2,32,24,128]{3,2,1,0:T(8,128)S(1)}, f32[384,128]{1,0:T(8,128)S(1)}, f32[384,128]{1,0:T(8,128)S(1)}) custom-call(bf16[16,6144]{1,0:T(8,128)(2,1)S(1)} %copy-done, bf16[256,256]{1,0:T(8,128)(2,1)S(1)} %pad_maximum_fusion.table, s32[1]{0:T(128)S(6)} %copy.6.seed), custom_call_target="tpu_custom_call" | custom-call | tf_op jit(solution)/shard_map/sums/pallas_call | solution.py:217
  45.8 4.7 %modes.1 = (f32[512,128]{1,0:T(8,128)}, f32[2,16,16,128]{3,2,1,0:T(8,128)}) custom-call(f32[2,768,128]{2,1,0:T(8,128)S(1)} %bitcast.4, f32[384,128]{1,0:T(8,128)S(1)} %get-tuple-element.8.sre, f32[384,128]{1,0:T(8,128)S(1)} %get-tuple-element.9.sim), custom_call_target="tpu_custom_call" | custom-call | tf_op jit(solution)/shard_map/modes/pallas_call | solution.py:373
  (3 shorter events, 0.1 us)
Async XLA Ops:
  2.0 0.9 %copy-start = (bf16[16,6144]{1,0:T(8,128)(2,1)S(1)}, bf16[16,6144]{1,0:T(8,128)(2,1)}, u32[]{:S(2)}) copy-start(bf16[16,6144]{1,0:T(8,128)(2,1)} %strain.1) | copy-start | bytes 589828

commit v6 on v5

--- a/solution.py
+++ b/solution.py
@@ -134,8 +134,6 @@
                 row = s * 2 * SKETCH + half * SKETCH
                 put(0, row, value)
 
-    pl.semaphore_wait(barrier, units + nz // 2 - 1)
-
     def landed(ref, sem):
         pltpu.make_async_copy(ref, ref, sem).wait()
 
@@ -143,11 +141,6 @@
         span = pl.ds(q, count)
         return remote(part.at[half, span], crecv.at[span], c_send, c_recv, mate)
 
-    @pl.when(core == 1)
-    def _():
-        pair(0, 0, units).start()
-
-    sent = units
     for t0 in range(SEGMENTS - 4, -1, -4):
         n = 8 * (t0 // 8 + 1)
         zero = jnp.zeros((n, LINES), jnp.float32)
@@ -165,13 +158,8 @@
                 for tile in range(n // 8):
                     row = gram_row(t0 + a, 8 * tile, half)
                     put(1, row, accs[2 * a + half][8 * tile:8 * tile + 8, :])
-        first = -(-gram_row(t0, 0, 0) // rows)
-
-        if first < sent:
-            @pl.when(core == 0)
-            def _(first=first, count=sent - first):
-                pair(1, first, count).start()
-        sent = min(sent, first)
+    pl.semaphore_wait(barrier, units + nz // 2 - 1)
+    pair(1 - core, 0, units).start()
 
     landed(crecv, c_recv)
     for d in far_first:

time: 50.7 us -> 49.7 us (0.980)
  Pallas kernels: 47.6 us -> 46.6 us
    pallas_call x1, Pallas kernels: 42.9 us -> 41.8 us  [all_sums(): pl.pallas_call(functools.partial(sum_kernel, dims), out_shape=[jax.ShapeD...]
where the time goes in v6:
time: 49.7 us; the launch traced here: 49.5 us
  Pallas kernels  46.6 us (94%)
  between operations  1.96 us (4%)
  other arithmetic  0.62 us (1%)
    pallas_call x1, Pallas kernels, all_sums(): pl.pallas_call(functools.partial(sum_kernel, dims), out_shape=[jax.ShapeD...  41.8 us
    pallas_call x1, Pallas kernels, finish(): pl.pallas_call(kernel, out_shape=[jax.ShapeDtypeStruct((channels * 2 * SK...  4.73 us

profile of v6, /device:TPU:1, one launch (start us, length us, event | category | flops | bytes accessed | tf_op | source)
XLA Modules:
  0.0 49.5 jit_solution(10787206471464555923)
XLA Ops:
  2.0 0.0 copy-start
  2.0 0.6 %multiply_convert_fusion.1 = (bf16[256,128]{1,0:T(8,128)(2,1)S(1)}, bf16[256,128]{1,0:T(8,128)(2,1)S(1)}) fusion(s32[128]{0:T(128)S(1)} %iota_add_fusion, f32[256]{0:T(256)S(1)} %get-tuple-element.14, f32[256]{0:T(256)S(1)} %get-tuple-element.15), kind=kLoop, calls=%fused_computation.8 | loop fusion | flops 589824 | bytes 133632 | tf_op jit(solution)/shard_map/convert
  2.6 0.3 copy-done
  2.9 41.8 %sums.1 = (f32[2,32,24,128]{3,2,1,0:T(8,128)S(1)}, f32[384,128]{1,0:T(8,128)S(1)}, f32[384,128]{1,0:T(8,128)S(1)}) custom-call(bf16[16,6144]{1,0:T(8,128)(2,1)S(1)} %copy-done, bf16[256,256]{1,0:T(8,128)(2,1)S(1)} %pad_maximum_fusion.table, s32[1]{0:T(128)S(6)} %copy.6.seed), custom_call_target="tpu_custom_call" | custom-call | tf_op jit(solution)/shard_map/sums/pallas_call | solution.py:205
  44.8 4.7 %modes.1 = (f32[512,128]{1,0:T(8,128)}, f32[2,16,16,128]{3,2,1,0:T(8,128)}) custom-call(f32[2,768,128]{2,1,0:T(8,128)S(1)} %bitcast.4, f32[384,128]{1,0:T(8,128)S(1)} %get-tuple-element.8.sre, f32[384,128]{1,0:T(8,128)S(1)} %get-tuple-element.9.sim), custom_call_target="tpu_custom_call" | custom-call | tf_op jit(solution)/shard_map/modes/pallas_call | solution.py:361
  (3 shorter events, 0.1 us)
Async XLA Ops:
  2.0 0.9 %copy-start = (bf16[16,6144]{1,0:T(8,128)(2,1)S(1)}, bf16[16,6144]{1,0:T(8,128)(2,1)}, u32[]{:S(2)}) copy-start(bf16[16,6144]{1,0:T(8,128)(2,1)} %strain.1) | copy-start | bytes 589828

commit v7 on v6

--- a/solution.py
+++ b/solution.py
@@ -83,6 +83,7 @@
         dx, dy = d // 2 // ny, d // 2 % ny
         return min(dx, nx - dx) + min(dy, ny - dy) + d % 2
 
+    level_order = sorted(range(1, nz // 2), key=lambda e: (-min(e, nz // 2 - e), e))
     far_first = sorted(range(1, units), key=lambda d: (-hops(d), d))
 
     def unit_device(u):
@@ -92,7 +93,7 @@
         return p * (2 * nz) + (lax.rem(level + e, nz // 2) * 2 + odd) * 2 + core
 
     barrier = pltpu.get_barrier_semaphore()
-    for e in range(1, nz // 2):
+    for e in level_order:
         pl.semaphore_signal(barrier, inc=1, device_id=(level_device(e),), device_id_type=MESH)
     for d in far_first:
         pl.semaphore_signal(barrier, inc=1, device_id=(unit_device(unit_at(d, 1)),), device_id_type=MESH)
@@ -171,7 +172,7 @@
     for d in range(1, units):
         total = total + xrecv[d]
     zall[level] = total
-    for e in range(1, nz // 2):
+    for e in level_order:
         remote(zall.at[level], zall.at[level], z_send, z_recv, level_device(e)).start()
     landed(zall.at[pl.ds(1, nz // 2 - 1)], z_recv)
     total = zall[0]

time: 49.7 us -> 49.6 us (level)
  no operation moved by 1% of the time
where the time goes in v7:
time: 49.6 us; the launch traced here: 49.5 us
  Pallas kernels  46.5 us (94%)
  between operations  1.96 us (4%)
  other arithmetic  0.62 us (1%)
    pallas_call x1, Pallas kernels, all_sums(): pl.pallas_call(functools.partial(sum_kernel, dims), out_shape=[jax.ShapeD...  41.8 us
    pallas_call x1, Pallas kernels, finish(): pl.pallas_call(kernel, out_shape=[jax.ShapeDtypeStruct((channels * 2 * SK...  4.73 us

profile of v7, /device:TPU:1, one launch (start us, length us, event | category | flops | bytes accessed | tf_op | source)
XLA Modules:
  0.0 49.5 jit_solution(9977168061666945841)
XLA Ops:
  2.0 0.0 copy-start
  2.0 0.6 %multiply_convert_fusion.1 = (bf16[256,128]{1,0:T(8,128)(2,1)S(1)}, bf16[256,128]{1,0:T(8,128)(2,1)S(1)}) fusion(s32[128]{0:T(128)S(1)} %iota_add_fusion, f32[256]{0:T(256)S(1)} %get-tuple-element.14, f32[256]{0:T(256)S(1)} %get-tuple-element.15), kind=kLoop, calls=%fused_computation.8 | loop fusion | flops 589824 | bytes 133632 | tf_op jit(solution)/shard_map/convert
  2.6 0.3 copy-done
  2.9 41.8 %sums.1 = (f32[2,32,24,128]{3,2,1,0:T(8,128)S(1)}, f32[384,128]{1,0:T(8,128)S(1)}, f32[384,128]{1,0:T(8,128)S(1)}) custom-call(bf16[16,6144]{1,0:T(8,128)(2,1)S(1)} %copy-done, bf16[256,256]{1,0:T(8,128)(2,1)S(1)} %pad_maximum_fusion.table, s32[1]{0:T(128)S(6)} %copy.6.seed), custom_call_target="tpu_custom_call" | custom-call | tf_op jit(solution)/shard_map/sums/pallas_call | solution.py:206
  44.7 4.7 %modes.1 = (f32[512,128]{1,0:T(8,128)}, f32[2,16,16,128]{3,2,1,0:T(8,128)}) custom-call(f32[2,768,128]{2,1,0:T(8,128)S(1)} %bitcast.4, f32[384,128]{1,0:T(8,128)S(1)} %get-tuple-element.8.sre, f32[384,128]{1,0:T(8,128)S(1)} %get-tuple-element.9.sim), custom_call_target="tpu_custom_call" | custom-call | tf_op jit(solution)/shard_map/modes/pallas_call | solution.py:362
  (3 shorter events, 0.1 us)
Async XLA Ops:
  2.0 0.9 %copy-start = (bf16[16,6144]{1,0:T(8,128)(2,1)S(1)}, bf16[16,6144]{1,0:T(8,128)(2,1)}, u32[]{:S(2)}) copy-start(bf16[16,6144]{1,0:T(8,128)(2,1)} %strain.1) | copy-start | bytes 589828

commit v8 on v7

--- a/solution.py
+++ b/solution.py
@@ -145,20 +145,24 @@
     for t0 in range(SEGMENTS - 4, -1, -4):
         n = 8 * (t0 // 8 + 1)
         zero = jnp.zeros((n, LINES), jnp.float32)
-        accs = [zero] * 8
+        accs = [zero] * 12
         for c in range(channels):
             vre = sre[pl.ds(c, n, stride=channels), :]
             vim = sim[pl.ds(c, n, stride=channels), :]
+            vdiff = vre - vim
             for a in range(4):
                 bre = sre[(t0 + a) * channels + c:(t0 + a) * channels + c + 1, :]
                 bim = sim[(t0 + a) * channels + c:(t0 + a) * channels + c + 1, :]
-                accs[2 * a] += vre * bre + vim * bim
-                accs[2 * a + 1] += vre * bim - vim * bre
+                accs[3 * a] += vre * bre
+                accs[3 * a + 1] += vim * bim
+                accs[3 * a + 2] += vdiff * (bre + bim)
         for a in range(4):
+            first, second, third = accs[3 * a:3 * a + 3]
+            value = (first + second, third - first + second)
             for half in range(2):
                 for tile in range(n // 8):
                     row = gram_row(t0 + a, 8 * tile, half)
-                    put(1, row, accs[2 * a + half][8 * tile:8 * tile + 8, :])
+                    put(1, row, value[half][8 * tile:8 * tile + 8, :])
     pl.semaphore_wait(barrier, units + nz // 2 - 1)
     pair(1 - core, 0, units).start()
 
@@ -186,13 +190,14 @@
         if d:
             remote(full.at[core, u], full.at[core, u], a_send, a_recv.at[d], unit_device(u)).wait_recv()
         remote(full.at[core, u], full.at[core, u], f_send, f_recv, mate).start()
+    full_out[core] = full[core]
     landed(full.at[1 - core], f_recv)
     landed(full.at[core], f_send)
     landed(crecv, c_send)
     landed(zall.at[pl.ds(1, nz // 2 - 1)], z_send)
     landed(xrecv.at[pl.ds(1, units - 1)], x_send)
     landed(xrecv.at[pl.ds(1, units - 1)], a_send)
-    full_out[...] = full[...]
+    full_out[1 - core] = full[1 - core]
 
 
 def all_sums(dims, strain, table, seed):

time: 49.6 us -> 49.6 us (level)
  no operation moved by 1% of the time
where the time goes in v8:
time: 49.6 us; the launch traced here: 49.4 us
  Pallas kernels  46.5 us (94%)
  between operations  1.96 us (4%)
  other arithmetic  0.62 us (1%)
    pallas_call x1, Pallas kernels, all_sums(): pl.pallas_call(functools.partial(sum_kernel, dims), out_shape=[jax.ShapeD...  41.8 us
    pallas_call x1, Pallas kernels, finish(): pl.pallas_call(kernel, out_shape=[jax.ShapeDtypeStruct((channels * 2 * SK...  4.73 us

profile of v8, /device:TPU:1, one launch (start us, length us, event | category | flops | bytes accessed | tf_op | source)
XLA Modules:
  0.0 49.4 jit_solution(6703032775520993506)
XLA Ops:
  2.0 0.0 copy-start
  2.0 0.6 %multiply_convert_fusion.1 = (bf16[256,128]{1,0:T(8,128)(2,1)S(1)}, bf16[256,128]{1,0:T(8,128)(2,1)S(1)}) fusion(s32[128]{0:T(128)S(1)} %iota_add_fusion, f32[256]{0:T(256)S(1)} %get-tuple-element.14, f32[256]{0:T(256)S(1)} %get-tuple-element.15), kind=kLoop, calls=%fused_computation.8 | loop fusion | flops 589824 | bytes 133632 | tf_op jit(solution)/shard_map/convert
  2.6 0.3 copy-done
  2.9 41.8 %sums.1 = (f32[2,32,24,128]{3,2,1,0:T(8,128)S(1)}, f32[384,128]{1,0:T(8,128)S(1)}, f32[384,128]{1,0:T(8,128)S(1)}) custom-call(bf16[16,6144]{1,0:T(8,128)(2,1)S(1)} %copy-done, bf16[256,256]{1,0:T(8,128)(2,1)S(1)} %pad_maximum_fusion.table, s32[1]{0:T(128)S(6)} %copy.6.seed), custom_call_target="tpu_custom_call" | custom-call | tf_op jit(solution)/shard_map/sums/pallas_call | solution.py:211
  44.7 4.7 %modes.1 = (f32[512,128]{1,0:T(8,128)}, f32[2,16,16,128]{3,2,1,0:T(8,128)}) custom-call(f32[2,768,128]{2,1,0:T(8,128)S(1)} %bitcast.4, f32[384,128]{1,0:T(8,128)S(1)} %get-tuple-element.8.sre, f32[384,128]{1,0:T(8,128)S(1)} %get-tuple-element.9.sim), custom_call_target="tpu_custom_call" | custom-call | tf_op jit(solution)/shard_map/modes/pallas_call | solution.py:367
  (3 shorter events, 0.1 us)
Async XLA Ops:
  2.0 0.9 %copy-start = (bf16[16,6144]{1,0:T(8,128)(2,1)S(1)}, bf16[16,6144]{1,0:T(8,128)(2,1)}, u32[]{:S(2)}) copy-start(bf16[16,6144]{1,0:T(8,128)(2,1)} %strain.1) | copy-start | bytes 589828
